TPU v7x, 32 devices: a whole 2x2x4 slice. The times are simulated.
32 devices in a mesh: ifg: 16 (over z, y, x), tile: 2 (over core).
Axes of the slice: x: 2, y: 2, z: 4, core: 2. Of those that a mesh axis runs over, the one named last changes fastest.
Arguments:
- phases: float32 [1024, 128, 64], P('ifg', 'tile'), may hold values from -6 to 6
- pairs: int32 [1024, 2], replicated, may hold values from 0 to 299, as said below
- class_weights: float32 [8, 1024], replicated, may hold values from 0.05 to 1
- classes: int32 [128, 64], P('tile', 'ifg'), may hold values from 0 to 7
Outputs:
- corrected: float32 [128, 64, 300], P('tile', 'ifg')
Inputs may be any that keep to these rules, and one draw needn't show every extreme that they name: pairs[i,0] < pairs[i,1] <= pairs[i,0] + 8; some interferogram starts at date 0 and some ends at date 300 - 1.
All inputs are finite; a program needn't handle non-finite values.
Results may differ from a plain program's by a relative error of at most 0.0003.
Values sent between devices are 32-bit elements; how exact they have to be, the bound alone decides.
A program may use at most 128 MiB of HBM per device.

v0:
```python
import functools
import math
import jax
import jax.numpy as jnp
from jax import lax
from jax.experimental import pallas as pl
from jax.experimental.pallas import tpu as pltpu
from jax.sharding import PartitionSpec as P

DATES = 300
CLASSES = 8
MAXGAP = 8
R = 3
LANES = 128
PAD = -(-DATES // 8) * 8
CHUNKS = 4
MESH = pl.DeviceIdType.MESH
HIGHEST = lax.Precision.HIGHEST

smooth_weight = 1.0
anchor_weight = 0.1


def split3(value):
    high = value.astype(jnp.bfloat16)
    rest = value - high.astype(jnp.float32)
    middle = rest.astype(jnp.bfloat16)
    low = (rest - middle.astype(jnp.float32)).astype(jnp.bfloat16)
    return (high, middle, low)


def dot_nt(a, b, **kw):
    return lax.dot_general(a, b, (((1,), (1,)), ((), ())), preferred_element_type=jnp.float32, **kw)


def dot_nn(a, b, **kw):
    return lax.dot_general(a, b, (((1,), (0,)), ((), ())), preferred_element_type=jnp.float32, **kw)


def factor(pairs_ref, w_ref, wt_ref, cls_ref, inc_ref, wpx_ref, lpx_ref, band, low):
    nifg = pairs_ref.shape[1]
    pixels = cls_ref.shape[1]
    first = pairs_ref[0:1, :]
    second = pairs_ref[1:2, :]
    gap = second - first
    dates = lax.broadcasted_iota(jnp.int32, (PAD, nifg), 0)
    minus_f = jnp.where(dates == first, 1.0, 0.0)
    plus_f = jnp.where(dates == second, 1.0, 0.0)
    inc_ref[...] = (plus_f - minus_f).astype(jnp.bfloat16)
    minus = minus_f.astype(jnp.bfloat16)
    both = (plus_f + minus_f).astype(jnp.bfloat16)
    w = w_ref[...]
    row = lax.broadcasted_iota(jnp.int32, (PAD, LANES), 0)
    inside = lambda ok: jnp.where(ok, 1.0, 0.0)
    for g in range(MAXGAP + 1):
        parts = split3(w if g == 0 else jnp.where(gap == g, w, 0.0))
        left = both if g == 0 else minus
        total = dot_nt(left, parts[0]) + (dot_nt(left, parts[1]) + dot_nt(left, parts[2]))
        here = inside(row <= DATES - 3)
        before = inside((row >= 1) & (row <= DATES - 2))
        if g == 0:
            twice = inside((row >= 2) & (row <= DATES - 1))
            prior = smooth_weight * (here + 4.0 * before + twice) + anchor_weight
            total = total + jnp.where(row < DATES, prior, 1.0)
        elif g == 1:
            total = smooth_weight * (-2.0 * here - 2.0 * before) - total
        elif g == 2:
            total = smooth_weight * here - total
        else:
            total = -total
        band[g] = total

    zero = jnp.zeros((1, LANES), jnp.float32)
    keys = [(j, h) for j in range(MAXGAP) for h in range(MAXGAP - j)]

    def factor_block(block, carry):
        acc = dict(zip(keys, carry))
        base = pl.multiple_of(block * 8, 8)
        for s in range(8):
            at = pl.ds(base + s, 1)
            c = [band[h, at, :] for h in range(MAXGAP + 1)]
            c = [c[h] - acc[(0, h)] for h in range(MAXGAP)] + [c[MAXGAP]]
            inv = 1.0 / c[0]
            low[0, at, :] = inv
            fresh = {}
            for j in range(1, MAXGAP + 1):
                lj = c[j] * inv
                low[j, at, :] = lj
                for h in range(MAXGAP - j + 1):
                    term = lj * c[j + h]
                    old = acc.get((j, h))
                    fresh[(j - 1, h)] = term if old is None else old + term
            acc = fresh
        return tuple(acc[k] for k in keys)

    lax.fori_loop(0, PAD // 8, factor_block, tuple(zero for _ in keys))

    member = lax.broadcasted_iota(jnp.int32, (LANES, pixels), 0)
    onehot = jnp.where(member == cls_ref[...], 1.0, 0.0).astype(jnp.bfloat16)

    def expand(value):
        parts = split3(value)
        return dot_nn(parts[0], onehot) + (dot_nn(parts[1], onehot) + dot_nn(parts[2], onehot))

    for g in range(MAXGAP + 1):
        lpx_ref[g] = expand(low[g])
    wpx_ref[...] = expand(wt_ref[...])


NORM = sum(math.exp(-j * j / 4.5) for j in range(-R, R + 1))


def tap(delta):
    near = jnp.exp((delta * delta).astype(jnp.float32) * (-1.0 / 4.5)) * (1.0 / NORM)
    return jnp.where(jnp.abs(delta) <= R, near, 0.0)


def split_index(index, size):
    if size & (size - 1):
        return index // size, index % size
    return index >> (size.bit_length() - 1), index & (size - 1)


def iota(shape, dim):
    return lax.broadcasted_iota(jnp.int32, shape, dim)


def fill_filters(tile_rows, tile_cols, own_ref, left_ref, right_ref, sel_ref, tile_ref):
    pixels = tile_rows * tile_cols
    me, core = lax.axis_index("ifg"), lax.axis_index("tile")
    count = lax.axis_size("ifg")
    has_left = jnp.where(me > 0, 1.0, 0.0)
    has_right = jnp.where(me < count - 1, 1.0, 0.0)
    square = (pixels, pixels)
    out_r, out_c = split_index(iota(square, 0), tile_cols)
    in_c, in_r = split_index(iota(square, 1), tile_rows)
    vertical = tap(out_r - in_r)
    same = jnp.where((out_r == in_r) & (out_c == in_c), 1.0, 0.0)
    own_ref[...] = same - vertical * tap(out_c - in_c)
    from_left = jnp.where(in_c >= 2, 1, in_c + 2)
    from_right = jnp.where(in_c >= 2, 2, in_c)
    left = -has_left * vertical * tap(out_c - from_left + tile_cols)
    right = -has_right * vertical * tap(out_c - from_right - tile_cols)
    for ref, value in ((left_ref, left), (right_ref, right)):
        parts = split3(value)
        ref[0] = parts[0]
        ref[1] = parts[1]
    slot_c, slot_j = split_index(iota((16, pixels), 0), 4)
    sel_c, sel_r = split_index(iota((16, pixels), 1), tile_rows)
    sent_r = jnp.where(core == 0, tile_rows - R, 0) + slot_j
    sel_ref[...] = jnp.where((slot_j < R) & (sent_r == sel_r) & (slot_c == sel_c), 1.0, 0.0)
    side, slot = split_index(iota((pixels, 48), 1), 16)
    slot_c, slot_j = split_index(slot, 4)
    out_r, out_c = split_index(iota((pixels, 48), 0), tile_cols)
    got_r = jnp.where(core == 0, tile_rows, -R) + slot_j
    reach = jnp.where(slot_j < R, tap(out_r - got_r), 0.0)
    has = jnp.where(side == 0, has_left, jnp.where(side == 1, 1.0, has_right))
    tile_ref[...] = -has * reach * tap(out_c - slot_c + (1 - side) * tile_cols)


def kernel(tile_rows, tile_cols, blocks_ref, pairs_ref, w_ref, wt_ref, cls_ref, out_ref,
           recv, inc_ref, wpx_ref, lpx_ref, band, low, own_ref, left_ref, right_ref, sel_ref,
           tile_ref, rows, x_ref, spare, edge, halo_pair, halo_spare, halo_tile,
           all_send, all_recv, own_sem, send_sem, recv_sem):
    me = lax.axis_index("ifg")
    core = lax.axis_index("tile")
    count = lax.axis_size("ifg")
    left = lax.rem(me + count - 1, count)
    right = lax.rem(me + 1, count)
    other = 1 - core
    near = [(me, other), (left, other), (right, other)]
    barrier = pltpu.get_barrier_semaphore()

    def greet(k, _):
        pl.semaphore_signal(barrier, inc=1, device_id=(lax.rem(me + k, count), core), device_id_type=MESH)
        return _

    lax.fori_loop(1, count, greet, 0)
    for partner in near:
        pl.semaphore_signal(barrier, inc=1, device_id=partner, device_id_type=MESH)
    pl.semaphore_wait(barrier, count - 1 + len(near))

    def exchange(k, slot):
        peer = lax.rem(me + k, count)
        return pltpu.make_async_remote_copy(
            src_ref=blocks_ref.at[peer], dst_ref=recv.at[slot], send_sem=all_send.at[k],
            recv_sem=all_recv.at[k], device_id=(peer, core), device_id_type=MESH)

    def send_block(k, _):
        exchange(k, me).start()
        return _

    lax.fori_loop(1, count, send_block, 0)
    mine = pltpu.make_async_copy(blocks_ref.at[me], recv.at[me], own_sem)
    mine.start()

    factor(pairs_ref, w_ref, wt_ref, cls_ref, inc_ref, wpx_ref, lpx_ref, band, low)
    fill_filters(tile_rows, tile_cols, own_ref, left_ref, right_ref, sel_ref, tile_ref)

    def take_block(k, _):
        exchange(k, lax.rem(me + count - k, count)).wait()
        return _

    mine.wait()
    lax.fori_loop(1, count, take_block, 0)

    pixels = x_ref.shape[1]
    parts = split3(recv[...].reshape(-1, pixels) * wpx_ref[...])
    inc = inc_ref[...]
    rows[0:PAD, :] = dot_nn(inc, parts[0]) + dot_nn(inc, parts[1])
    rows[PAD:PAD + 8, :] = jnp.zeros((8, pixels), jnp.float32)

    def forward(block, carry):
        a = list(carry)
        base = pl.multiple_of(block * 8, 8)
        for s in range(8):
            at = pl.ds(base + s, 1)
            y = a[0]
            a = a[1:] + [rows[pl.ds(base + s + 8, 1), :]]
            a = [a[j] - lpx_ref[j + 1, at, :] * y for j in range(8)]
            x_ref[at, :] = y * lpx_ref[0, at, :]
        return tuple(a)

    lax.fori_loop(0, PAD // 8, forward, tuple(rows[d:d + 1, :] for d in range(8)))

    def backward(block, carry):
        later = list(carry)
        base = pl.multiple_of(block * 8, 8)
        for s in range(7, -1, -1):
            at = pl.ds(base + s, 1)
            value = x_ref[at, :]
            for g in range(8, 0, -1):
                value = value - lpx_ref[g, at, :] * later[g - 1]
            x_ref[at, :] = value
            later = [value] + later[:7]
        return tuple(later)

    def copy(i, src, dst, device):
        return pltpu.make_async_remote_copy(src_ref=src, dst_ref=dst, send_sem=send_sem.at[i],
                                            recv_sem=recv_sem.at[i], device_id=device,
                                            device_id_type=MESH)

    has_left, has_right = me > 0, me < count - 1

    @pl.when(jnp.logical_not(has_left))
    def _():
        halo_pair[0] = jnp.zeros_like(halo_pair[0])
        halo_spare[0] = jnp.zeros_like(halo_spare[0])
        halo_tile[0] = jnp.zeros_like(halo_tile[0])

    @pl.when(jnp.logical_not(has_right))
    def _():
        halo_pair[1] = jnp.zeros_like(halo_pair[1])
        halo_spare[1] = jnp.zeros_like(halo_spare[1])
        halo_tile[2] = jnp.zeros_like(halo_tile[2])

    half = pixels // 2
    total_blocks = PAD // 8
    cuts = [total_blocks * (CHUNKS - i) // CHUNKS for i in range(CHUNKS + 1)]
    carry = tuple(jnp.zeros((1, pixels), jnp.float32) for _ in range(8))
    to_left, to_right = [], []
    for i in range(CHUNKS):
        top, bottom = cuts[i], cuts[i + 1]
        carry = lax.fori_loop(0, top - bottom, lambda n, c, top=top: backward(top - 1 - n, c), carry)
        span = pl.ds(bottom * 8, (top - bottom) * 8)
        to_left.append(copy(2 * i, x_ref.at[span, pl.ds(0, half)], halo_pair.at[1, span], (left, core)))
        to_right.append(copy(2 * i + 1, x_ref.at[span, pl.ds(half, half)], halo_pair.at[0, span], (right, core)))
        if i < CHUNKS - 1:
            pl.when(has_left)(to_left[-1].start)
            pl.when(has_right)(to_right[-1].start)
    x = x_ref[...]
    edge[...] = dot_nt(sel_ref[...], x, precision=HIGHEST)
    small = [copy(2 * CHUNKS + 2 + i, edge, halo_tile.at[slot], near[i]) for i, slot in enumerate((1, 2, 0))]
    small[0].start()
    pl.when(has_left)(small[1].start)
    pl.when(has_right)(small[2].start)
    pl.when(has_left)(to_left[-1].start)
    pl.when(has_right)(to_right[-1].start)
    mid = PAD // 2
    low_lanes = iota((mid, half), 1) < half // 2
    first, second = x[:, 0:half], x[:, half:]
    spare[0] = jnp.where(low_lanes, pltpu.roll(first[0:mid], half // 2, 1), first[mid:])
    spare[1] = jnp.where(low_lanes, second[0:mid], pltpu.roll(second[mid:], half // 2, 1))
    to_right.append(copy(2 * CHUNKS, spare.at[0], halo_spare.at[0], (right, core)))
    to_left.append(copy(2 * CHUNKS + 1, spare.at[1], halo_spare.at[1], (left, core)))
    pl.when(has_right)(to_right[-1].start)
    pl.when(has_left)(to_left[-1].start)
    total = dot_nt(own_ref[...], x, precision=HIGHEST)
    small[0].wait()
    pl.when(has_left)(small[1].wait_send)
    pl.when(has_right)(small[1].wait_recv)
    pl.when(has_right)(small[2].wait_send)
    pl.when(has_left)(small[2].wait_recv)
    total += dot_nn(tile_ref[...], halo_tile[...].reshape(48, PAD), precision=HIGHEST)
    for c in to_right:
        pl.when(has_right)(c.wait_send)
        pl.when(has_left)(c.wait_recv)
    for c in to_left:
        pl.when(has_left)(c.wait_send)
        pl.when(has_right)(c.wait_recv)
    keep = (iota((PAD, half), 0) < mid) == (iota((PAD, half), 1) < half // 2)
    for side, ref in ((0, left_ref), (1, right_ref)):
        again = halo_spare[side]
        extra = jnp.where(keep, jnp.concatenate([again, again], axis=0), 0.0)
        high, middle, _ = split3(jnp.concatenate([halo_pair[side], extra], axis=1))
        total = total + (dot_nt(ref[0], high) + (dot_nt(ref[0], middle) + dot_nt(ref[1], high)))
    out_ref[...] = total[:, 0:DATES]


def on_device(phases, pairs, class_weights, classes):
    own_ifg, tile_rows, cols = phases.shape
    tile_cols = classes.shape[1]
    pixels = tile_rows * tile_cols
    count = cols // tile_cols
    nifg = pairs.shape[0]
    half = pixels // 2
    vmem = pl.BlockSpec(memory_space=pltpu.VMEM)
    f32, bf16 = jnp.float32, jnp.bfloat16
    copies = 2 * CHUNKS + 5

    blocks = phases.transpose(0, 2, 1).reshape(own_ifg, count, pixels).transpose(1, 0, 2)
    padded = jnp.pad(class_weights, ((0, LANES - CLASSES), (0, 0)))
    corrected = pl.pallas_call(
        functools.partial(kernel, tile_rows, tile_cols),
        out_shape=jax.ShapeDtypeStruct((pixels, DATES), f32),
        in_specs=[vmem] * 5,
        out_specs=vmem,
        scratch_shapes=[
            pltpu.VMEM((count, own_ifg, pixels), f32),
            pltpu.VMEM((PAD, nifg), bf16),
            pltpu.VMEM((nifg, pixels), f32),
            pltpu.VMEM((MAXGAP + 1, PAD, pixels), f32),
            pltpu.VMEM((MAXGAP + 1, PAD, LANES), f32),
            pltpu.VMEM((MAXGAP + 1, PAD, LANES), f32),
            pltpu.VMEM((pixels, pixels), f32),
            pltpu.VMEM((2, pixels, pixels), bf16),
            pltpu.VMEM((2, pixels, pixels), bf16),
            pltpu.VMEM((16, pixels), f32),
            pltpu.VMEM((pixels, 48), f32),
            pltpu.VMEM((PAD + 8, pixels), f32),
            pltpu.VMEM((PAD, pixels), f32),
            pltpu.VMEM((2, PAD // 2, half), f32),
            pltpu.VMEM((16, PAD), f32),
            pltpu.VMEM((2, PAD, half), f32),
            pltpu.VMEM((2, PAD // 2, half), f32),
            pltpu.VMEM((3, 16, PAD), f32),
            pltpu.SemaphoreType.DMA((count,)),
            pltpu.SemaphoreType.DMA((count,)),
            pltpu.SemaphoreType.DMA,
            pltpu.SemaphoreType.DMA((copies,)),
            pltpu.SemaphoreType.DMA((copies,)),
        ],
        compiler_params=pltpu.CompilerParams(
            collective_id=0, has_side_effects=True, vmem_limit_bytes=48 * 1024 * 1024
        ),
        name="invert_and_filter",
    )(blocks, pairs.T, padded, padded.T, classes.T.reshape(1, pixels))
    return corrected.reshape(tile_rows, tile_cols, DATES)


def solution(mesh):
    return jax.shard_map(
        on_device,
        mesh=mesh,
        in_specs=(P("ifg", "tile", None), P(), P(), P("tile", "ifg")),
        out_specs=P("tile", "ifg", None),
        check_vma=False,
    )
```

profile of v0, /device:TPU:10, one launch (start us, length us, event | category | flops | bytes accessed | tf_op | source)
XLA Modules:
  0.0 49.0 jit_solution(1743462845240308741)
XLA Ops:
  0.0 1.9 %copy.7 = f32[64,64,64]{2,1,0:T(8,128)S(1)} copy(f32[64,64,64]{1,2,0:T(8,128)} %bitcast.10) | data formatting | bytes 2097152 | tf_op jit(solution)/shard_map/transpose | solution.py:321
  1.9 0.0 copy-start.1
  1.9 0.5 %reshape.9 = f32[64,16,256]{2,1,0:T(8,128)S(1)} reshape(f32[64,64,64]{2,1,0:T(8,128)S(1)} %copy.7) | data formatting | bytes 2097152 | tf_op jit(solution)/shard_map/reshape | solution.py:321
  2.5 0.0 copy-start.2
  2.5 0.0 copy-start
  2.5 0.6 %copy.13 = f32[64,16,256]{2,0,1:T(8,128)S(1)} copy(f32[64,16,256]{2,1,0:T(8,128)S(1)} %reshape.9) | data formatting | bytes 2097152 | tf_op jit(solution)/shard_map/reshape | solution.py:321
  3.1 0.0 copy-done.1
  3.1 0.2 copy.9
  3.3 0.2 copy.12
  3.5 0.1 pad.4.clone.w_ref
  3.6 0.0 copy-done.2
  3.6 0.1 reshape.10.cls_ref
  3.7 0.0 copy-done
  3.7 44.4 %invert_and_filter.1 = f32[256,300]{1,0:T(8,128)S(1)} custom-call(f32[16,64,256]{2,1,0:T(8,128)S(1)} %bitcast.8, s32[2,1024]{1,0:T(2,128)S(1)} %bitcast.9, f32[128,1024]{1,0:T(8,128)S(1)} %pad.4.clone.w_ref, f32[1024,128]{1,0:T(8,128)S(1)} %pad_bitcast_fusion.wt_ref, s32[1,256]{1,0:T(1,128)S(1)} %reshape.10.cls_ref), custom_call_target="tpu_custom_call" | custom-call | tf_op jit(solution)/shard_map/invert_and_filter/pallas_call | solution.py:323
  48.1 0.9 %reshape.11 = f32[64,4,300]{2,1,0:T(4,128)} reshape(f32[256,300]{1,0:T(8,128)S(1)} %invert_and_filter.1) | data formatting | bytes 614400 | tf_op jit(solution)/shard_map/reshape | solution.py:358
  (1 shorter events, 0.0 us)
Async XLA Ops:
  1.9 1.2 %copy-start.1 = (f32[8,1024]{1,0:T(8,128)S(1)}, f32[8,1024]{1,0:T(8,128)}, u32[]{:S(2)}) copy-start(f32[8,1024]{1,0:T(8,128)} %param.6) | copy-start | bytes 98308
  2.5 1.1 %copy-start.2 = (s32[64,4]{0,1:T(4,128)S(1)}, s32[64,4]{0,1:T(4,128)}, u32[]{:S(2)}) copy-start(s32[64,4]{0,1:T(4,128)} %param.7) | copy-start | bytes 3076
  2.5 1.2 %copy-start = (s32[1024,2]{0,1:T(2,128)S(1)}, s32[1024,2]{0,1:T(2,128)}, u32[]{:S(2)}) copy-start(s32[1024,2]{0,1:T(2,128)} %param.5) | copy-start | bytes 24580
where the time goes:
time: 49.1 us; the launch traced here: 49 us
  Pallas kernels  44.4 us (90%)
  local copies, waits for them, and re-layouts  4.47 us (9%)
    pallas_call x1, Pallas kernels, on_device(): pl.pallas_call(functools.partial(kernel, tile_rows, tile_cols), out_shape...  44.4 us
    transpose x1, local copies, waits for them, and re-layouts, on_device(): phases.transpose(0, 2, 1).reshape(own_ifg, count, pixels).transpose(1, 0, 2)  1.92 us
    reshape x2, local copies, waits for them, and re-layouts, on_device(): phases.transpose(0, 2, 1).reshape(own_ifg, count, pixels).transpose(1, 0, 2)  1.14 us

commit v1 on v0

v1 whole, which is shorter than its diff:
```python
import functools
import math
import jax
import jax.numpy as jnp
from jax import lax
from jax.experimental import pallas as pl
from jax.experimental.pallas import tpu as pltpu
from jax.sharding import PartitionSpec as P

DATES = 300
CLASSES = 8
MAXGAP = 8
R = 3
LANES = 128
HALF = DATES // 2
MEET = HALF - MAXGAP // 2
LAST = MEET + MAXGAP
ROWS = -(-LAST // 16) * 16
OUT = -(-HALF // 8) * 8
CUT = (OUT // 16) * 8
BLOCKS = MEET // 8
PARTS = ((1, 2), (0, 3))
MESH = pl.DeviceIdType.MESH

smooth_weight = 1.0
anchor_weight = 0.1

NORM = sum(math.exp(-j * j / 4.5) for j in range(-R, R + 1))
F32, BF16 = jnp.float32, jnp.bfloat16


def split3(value):
    high = value.astype(BF16)
    rest = value - high.astype(F32)
    middle = rest.astype(BF16)
    low = (rest - middle.astype(F32)).astype(BF16)
    return (high, middle, low)


def split2(value):
    high = value.astype(BF16)
    return high, (value - high.astype(F32)).astype(BF16)


def dot_nt(a, b):
    return lax.dot_general(a, b, (((1,), (1,)), ((), ())), preferred_element_type=F32)


def dot_nn(a, b):
    return lax.dot_general(a, b, (((1,), (0,)), ((), ())), preferred_element_type=F32)


def iota(shape, dim):
    return lax.broadcasted_iota(jnp.int32, shape, dim)


def one(cond):
    return jnp.where(cond, 1.0, 0.0)


def tap(delta):
    near = jnp.exp((delta * delta).astype(F32) * (-1.0 / 4.5)) * (1.0 / NORM)
    return jnp.where(jnp.abs(delta) <= R, near, 0.0)


def tap_at(delta):
    return math.exp(-delta * delta / 4.5) / NORM if abs(delta) <= R else 0.0


def swap(value):
    return pltpu.roll(value, LANES // 2, 1)


def bands(pairs_ref, w_ref, band):
    nifg = pairs_ref.shape[1]
    first, second = pairs_ref[0:1, :], pairs_ref[1:2, :]
    gap = second - first
    row = iota((ROWS, nifg), 0)
    left = [one(row == first), one(row == second), one(DATES - 1 - row == second), one(DATES - 1 - row == first)]
    left = jnp.concatenate(left, axis=0).astype(BF16)
    w = w_ref[...]
    zero = jnp.zeros((CLASSES, nifg), F32)
    grouped = [jnp.where(gap == g, w, 0.0) for g in range(1, MAXGAP + 1)] + [w] + [zero] * 7
    high, middle, low = split3(jnp.concatenate(grouped, axis=0))
    both = dot_nt(left, jnp.concatenate([high, middle], axis=0))
    total = both[:, :LANES] + (both[:, LANES:] + dot_nt(left, low))
    ff, fs, bs, bf = [total[i * ROWS:(i + 1) * ROWS] for i in range(4)]
    lane = iota((ROWS, LANES), 1)
    t = iota((ROWS, LANES), 0)
    front, used = lane < LANES // 2, (lane & (LANES // 2 - 1)) < CLASSES
    band[0] = jnp.where(used, jnp.where(front, swap(ff + fs), bs + bf), 0.0) + (
        smooth_weight * (1.0 + 4.0 * one(t >= 1) + one(t >= 2)) + anchor_weight)
    off = jnp.where(front, ff, swap(bs))
    for g in range(1, MAXGAP + 1):
        here = off if g == 1 else pltpu.roll(off, LANES - 8 * (g - 1), 1)
        here = -jnp.where(used, here, 0.0)
        if g == 1:
            here += smooth_weight * (-2.0 - 2.0 * one(t >= 1))
        elif g == 2:
            here += smooth_weight
        band[g] = jnp.where(t + g < LAST, here, 0.0)


def factor(band, low):
    zero = jnp.zeros((1, LANES), F32)
    keys = [(j, h) for j in range(MAXGAP) for h in range(MAXGAP - j)]

    def step(at, acc):
        c = [band[h, at, :] for h in range(MAXGAP + 1)]
        c = [c[h] - acc[(0, h)] for h in range(MAXGAP)] + [c[MAXGAP]]
        inv = 1.0 / c[0]
        low[0, at, :] = inv
        fresh = {}
        for j in range(1, MAXGAP + 1):
            lj = c[j] * inv
            low[j, at, :] = lj
            for h in range(MAXGAP - j + 1):
                term = lj * c[j + h]
                old = acc.get((j, h))
                fresh[(j - 1, h)] = term if old is None else old + term
        return fresh

    def block(b, carry):
        acc = dict(zip(keys, carry))
        base = pl.multiple_of(b * 8, 8)
        for s in range(8):
            acc = step(pl.ds(base + s, 1), acc)
        return tuple(acc[k] for k in keys)

    acc = dict(zip(keys, lax.fori_loop(0, BLOCKS, block, tuple(zero for _ in keys))))
    for t in range(8 * BLOCKS, MEET):
        acc = step(pl.ds(t, 1), acc)
    acc = {(j, h): acc[(j, h)] + swap(acc[(MAXGAP - 1 - j - h, h)]) for j, h in keys}
    for t in range(MEET, LAST):
        acc = step(pl.ds(t, 1), acc)


def prepare(pairs_ref, w_ref, cls_ref, per, count, inc_ref, wpx_ref, lpx_ref, band, low):
    nifg = pairs_ref.shape[1]
    half = nifg // 2
    q, lane = iota((LANES, LANES), 0), iota((LANES, LANES), 1)
    local = q & 63
    place = (local < 3 * CLASSES) & ((q >= 64) == (lane >= 64))
    classes = cls_ref[...]
    classes = jnp.concatenate([classes, classes], axis=1)
    onehot = [one(place & ((local & 7) == classes[c:c + 1, :])) for c in range(4)]
    onehot = jnp.concatenate(onehot, axis=1).astype(BF16)

    parts = [p.astype(F32) for p in split3(w_ref[...])]
    ends = [jnp.broadcast_to(pairs_ref[i:i + 1, :].astype(F32), (8, nifg)) for i in range(2)]
    stack = jnp.concatenate(parts + ends + [jnp.zeros((24, nifg), F32)], axis=0)
    by_ifg = jnp.concatenate([stack, stack], axis=0).T.reshape(count, 2 * per, LANES)
    ours, theirs = by_ifg[:, :per].reshape(half, LANES), by_ifg[:, per:].reshape(half, LANES)
    packed = jnp.where(iota((half, LANES), 1) < 64, ours, theirs)
    weights = dot_nn(packed.astype(BF16), onehot)
    for c in range(4):
        wpx_ref[c] = weights[:, c * LANES:(c + 1) * LANES]
    ends = packed.T
    row = iota((ROWS, half), 0)
    inside = row < HALF
    row = row.astype(F32)
    for h in range(2):
        first, second = ends[64 * h + 24:64 * h + 25, :], ends[64 * h + 32:64 * h + 33, :]
        front = one(inside & (row == second)) - one(inside & (row == first))
        back = one(inside & (DATES - 1.0 - row == second)) - one(inside & (DATES - 1.0 - row == first))
        inc_ref[h, 0:ROWS, :] = front.astype(BF16)
        inc_ref[h, ROWS:, :] = back.astype(BF16)

    bands(pairs_ref, w_ref, band)
    factor(band, low)
    used = (iota((ROWS, LANES), 1) & 63) < CLASSES
    valid = iota((ROWS, LANES), 0) < LAST
    for g in range(MAXGAP + 1):
        high, middle, rest = [p.astype(F32) for p in split3(jnp.where(used & valid, low[g], 0.0))]
        value = high + pltpu.roll(middle, 8, 1) + pltpu.roll(rest, 16, 1)
        each = dot_nn(value.astype(BF16), onehot)
        for p, columns in enumerate(PARTS):
            for i, c in enumerate(columns):
                lpx_ref[p, g, pl.ds(i, ROWS, stride=2), :] = each[:, c * LANES:(c + 1) * LANES]


def fill_filters(dirs, has_left, has_right, k_ref, sel_ref, tile_ref):
    shape = (2 * 256, LANES)
    row, lane = iota(shape, 0), iota(shape, 1)
    out_c, out_r = row & 3, (row & 255) >> 2
    match = (row >= 256) == (lane >= 64)
    delta = out_r - (lane & 63)
    vertical = jnp.where(match, tap(delta), 0.0)
    straight = one(match & (delta == 0))

    def column(at, has):
        taps = [tap_at(c - at) for c in range(4)]
        near = jnp.where(out_c == 0, taps[0], jnp.where(out_c == 1, taps[1], jnp.where(out_c == 2, taps[2], taps[3])))
        value = -vertical * near
        if 0 <= at < 4:
            value += jnp.where(out_c == at, straight, 0.0)
        return value if has is None else value * has

    sets = [(1, None, 2, None), (-3, has_left, -2, has_left), (5, has_right, 6, has_right), (0, None, 3, None), (-1, has_left, 4, has_right)]
    for i, (a, has_a, b, has_b) in enumerate(sets):
        high, middle = split2(jnp.concatenate([column(a, has_a), column(b, has_b)], axis=1))
        k_ref[i, 0] = high
        k_ref[i, 1] = middle
    for d, (_, _, sent, _) in enumerate(dirs):
        shape = (16, 2 * LANES)
        row, lane = iota(shape, 0), iota(shape, 1)
        pick = ((row >> 2) == (lane >> 6)) & ((row & 3) < R) & ((lane & 63) == sent + (row & 3))
        sel_ref[d] = one(pick).astype(BF16)
    for p, columns in enumerate(PARTS):
        for d, (_, has, _, got) in enumerate(dirs):
            shape = (2 * 256, 48)
            row, lane = iota(shape, 0), iota(shape, 1)
            side, slot = lane >> 4, lane & 15
            col = jnp.where((slot >> 3) == 0, columns[0], columns[1]) + 4 * (side - 1)
            out_c, out_r = row & 3, (row & 255) >> 2
            ok = ((slot & 3) < R) & (((slot >> 2) & 1) == (row >> 8))
            value = jnp.where(ok, -tap(out_r - got - (slot & 3)) * tap(out_c - col), 0.0)
            there = jnp.where(side == 0, has_left, jnp.where(side == 2, has_right, 1.0))
            value = value * there if has is None else value * there * one(has)
            high, middle = split2(value)
            tile_ref[p, d, 0] = high
            tile_ref[p, d, 1] = middle


def kernel(tile_rows, tiles, phases_ref, pairs_ref, w_ref, cls_ref, out_ref,
           phase, blocks, recv, inc_ref, wpx_ref, lpx_ref, band, low, k_ref, sel_ref, tile_ref,
           z_ref, y_ref, x_ref, edge, halo_one, halo_two, halo_tile, acc,
           load_sem, own_sem, all_send, all_recv, send_sem, recv_sem):
    me, core = lax.axis_index("ifg"), lax.axis_index("tile")
    count = lax.axis_size("ifg")
    own = phase.shape[0]
    per = own // 2
    cols = phase.shape[2]
    left, right = lax.rem(me + count - 1, count), lax.rem(me + 1, count)
    has_left, has_right = me > 0, me < count - 1
    if tiles == 2:
        dirs = [(1 - core, None, jnp.where(core == 0, tile_rows - R, 0), jnp.where(core == 0, tile_rows, -R))]
    else:
        dirs = [(lax.rem(core + tiles - 1, tiles), core > 0, 0, -R),
                (lax.rem(core + 1, tiles), core < tiles - 1, tile_rows - R, tile_rows)]

    pieces = 2
    loads = []
    for i in range(pieces):
        for h in range(2):
            span = pl.ds(h * per + i * (per // pieces), per // pieces)
            loads.append(pltpu.make_async_copy(phases_ref.at[span], phase.at[span], load_sem.at[2 * i + h]))
            loads[-1].start()

    barrier = pltpu.get_barrier_semaphore()

    def greet(k, _):
        pl.semaphore_signal(barrier, inc=1, device_id=(lax.rem(me + k, count), core), device_id_type=MESH)
        return _

    lax.fori_loop(1, count, greet, 0)
    near = [[(me, tile), (left, tile), (right, tile)] for tile, _, _, _ in dirs]
    for group in near:
        for partner in group:
            pl.semaphore_signal(barrier, inc=1, device_id=partner, device_id_type=MESH)

    for i in range(pieces):
        loads[2 * i].wait()
        loads[2 * i + 1].wait()

        def turn(q, _):
            value = jnp.concatenate([phase[q], phase[q + per]], axis=0).T
            blocks[pl.ds(q, cols, stride=per), :] = value
            return _

        lax.fori_loop(i * (per // pieces), (i + 1) * (per // pieces), turn, 0, unroll=4)
    pl.semaphore_wait(barrier, count - 1 + 3 * len(dirs))

    spans = [(per, 2 * per), (0, per), (3 * per, per)]

    def exchange(i, k, src):
        peer = lax.rem(me + k, count)
        at, size = spans[i]
        return pltpu.make_async_remote_copy(
            src_ref=blocks.at[pl.ds(pl.multiple_of(peer * 4 * per + at, 8), size)], dst_ref=recv.at[src, pl.ds(at, size)],
            send_sem=all_send.at[i, k], recv_sem=all_recv.at[i, k], device_id=(peer, core), device_id_type=MESH)

    for group in ((0,), (1, 2)):
        def send_blocks(k, _, group=group):
            for i in group:
                exchange(i, k, me).start()
            return _

        lax.fori_loop(1, count, send_blocks, 0)
    mine = pltpu.make_async_copy(blocks.at[pl.ds(pl.multiple_of(me * 4 * per, 8), 4 * per)], recv.at[me], own_sem)
    mine.start()

    def absent(cond, *refs):
        @pl.when(jnp.logical_not(cond))
        def _():
            for ref in refs:
                ref[...] = jnp.zeros(ref.shape, F32)

    absent(has_left, halo_one.at[0], halo_two.at[0])
    absent(has_right, halo_one.at[1], halo_two.at[1])
    for p in range(2):
        for d, (_, has, _, _) in enumerate(dirs):
            absent(has_left if has is None else has_left & has, halo_tile.at[p, d, 0])
            absent(has_right if has is None else has_right & has, halo_tile.at[p, d, 2])
            if has is not None:
                absent(has, halo_tile.at[p, d, 1])

    prepare(pairs_ref, w_ref, cls_ref, per, count, inc_ref, wpx_ref, lpx_ref, band, low)
    fill_filters(dirs, one(has_left), one(has_right), k_ref, sel_ref, tile_ref)
    mine.wait()

    def take(group):
        def take_blocks(k, _):
            for i in group:
                exchange(i, k, lax.rem(me + count - k, count)).wait_recv()
            return _

        lax.fori_loop(1, count, take_blocks, 0)

    low_lanes = iota((ROWS, LANES), 1) < LANES // 2

    def right_side(p):
        values = []
        for c in PARTS[p]:
            got = recv[:, c * per:(c + 1) * per, :].reshape(count * per, LANES)
            values.append(got * wpx_ref[c])
        high, middle = split2(jnp.concatenate(values, axis=1))
        a, b = [dot_nn(inc_ref[h], high) + dot_nn(inc_ref[h], middle) for h in range(2)]
        for i in range(2):
            at = slice(i * LANES, (i + 1) * LANES)
            aa, ab, ba, bb = a[:ROWS, at], a[ROWS:, at], b[:ROWS, at], b[ROWS:, at]
            z_ref[pl.ds(i, ROWS, stride=2), :] = jnp.where(low_lanes, aa, bb) + swap(jnp.where(low_lanes, ab, ba))

    def forward(p):
        def step(t, a):
            at = pl.ds(t, 2)
            y = a[0]
            y_ref[at, :] = y * lpx_ref[p, 0, at, :]
            return [v - lpx_ref[p, j + 1, at, :] * y for j, v in enumerate(a[1:])]

        def block(b, carry):
            a = list(carry)
            base = pl.multiple_of(b * 16, 16)
            for s in range(8):
                a = step(base + 2 * s, a + [z_ref[pl.ds(base + 2 * s + 16, 2), :]])
            return tuple(a)

        a = list(lax.fori_loop(0, BLOCKS, block, tuple(z_ref[2 * t:2 * t + 2, :] for t in range(8))))
        for t in range(8 * BLOCKS, MEET):
            a = step(2 * t, a + [z_ref[2 * t + 16:2 * t + 18, :]])
        a = [a[j] + swap(a[7 - j]) for j in range(8)]
        for t in range(MEET, LAST):
            a = step(2 * t, a)

    def backward(p, send):
        one_ref, two_ref = x_ref.at[PARTS[p][0]], x_ref.at[PARTS[p][1]]

        def step(t, later, keep=True):
            at = pl.ds(2 * t, 2)
            value = y_ref[at, :]
            for g in range(len(later), 0, -1):
                value = value - lpx_ref[p, g, at, :] * later[g - 1]
            if keep:
                one_ref[pl.ds(t, 1), :] = value[0:1]
                two_ref[pl.ds(t, 1), :] = value[1:2]
            return [value] + later[:7]

        later = []
        for t in range(LAST - 1, 8 * BLOCKS - 1, -1):
            later = step(t, later, t < OUT)

        def block(b, carry):
            later = list(carry)
            base = pl.multiple_of(b * 8, 8)
            for s in range(7, -1, -1):
                later = step(base + s, later)
            return tuple(later)

        cut = CUT // 8
        carry = lax.fori_loop(0, BLOCKS - cut, lambda n, c: block(BLOCKS - 1 - n, c), tuple(later))
        send(0, pl.ds(CUT, OUT - CUT))
        lax.fori_loop(0, cut, lambda n, c: block(cut - 1 - n, c), carry)
        send(1, pl.ds(0, CUT))

    def copy(i, src, dst, device):
        return pltpu.make_async_remote_copy(src_ref=src, dst_ref=dst, send_sem=send_sem.at[i],
                                            recv_sem=recv_sem.at[i], device_id=device, device_id_type=MESH)

    sides = [[], []]

    def send_one(piece, span):
        src = x_ref.at[pl.ds(1, 2), span]
        sides[0].append(copy(2 * piece, src, halo_one.at[1, :, span], (left, core)))
        sides[1].append(copy(2 * piece + 1, src, halo_one.at[0, :, span], (right, core)))
        pl.when(has_left)(sides[0][-1].start)
        pl.when(has_right)(sides[1][-1].start)

    def send_two(piece, span):
        sides[0].append(copy(4 + 2 * piece, x_ref.at[0, span], halo_two.at[1, span], (left, core)))
        sides[1].append(copy(5 + 2 * piece, x_ref.at[3, span], halo_two.at[0, span], (right, core)))
        pl.when(has_left)(sides[0][-1].start)
        pl.when(has_right)(sides[1][-1].start)

    edges = []

    def both(a, b):
        return b if a is None else a if b is None else a & b

    def when(cond, action):
        action() if cond is None else pl.when(cond)(action)

    def solved(p):
        value = jnp.concatenate([x_ref[c] for c in PARTS[p]], axis=1)
        return split3(value)

    def send_edges(p, parts):
        for d, (_, has, _, _) in enumerate(dirs):
            edge[p, d] = dot_nt(sel_ref[d], parts[0]) + (dot_nt(sel_ref[d], parts[1]) + dot_nt(sel_ref[d], parts[2]))
            opposite = len(dirs) - 1 - d
            got = dirs[opposite][1]
            for i, (slot, to, came) in enumerate(((1, None, None), (2, has_left, has_right), (0, has_right, has_left))):
                c = copy(8 + (p * len(dirs) + d) * 3 + i, edge.at[p, d], halo_tile.at[p, opposite, slot], near[d][i])
                edges.append((c, both(has, to), both(got, came)))
                when(edges[-1][1], c.start)

    def apply(i, parts):
        return dot_nt(k_ref[i, 0], parts[0]) + (dot_nt(k_ref[i, 0], parts[1]) + dot_nt(k_ref[i, 1], parts[0]))

    def apply_tile(p):
        total = None
        for d in range(len(dirs)):
            high, middle = split2(halo_tile[p, d].reshape(48, OUT))
            term = dot_nn(tile_ref[p, d, 0], high) + (dot_nn(tile_ref[p, d, 0], middle) + dot_nn(tile_ref[p, d, 1], high))
            total = term if total is None else total + term
        return total

    def wait_sides(first):
        for i in (2 * first, 2 * first + 1):
            pl.when(has_right)(sides[0][i].wait_recv)
            pl.when(has_left)(sides[1][i].wait_recv)

    take((0,))
    right_side(0)
    forward(0)
    backward(0, send_one)
    parts = solved(0)
    send_edges(0, parts)
    acc[...] = apply(0, parts)

    take((1, 2))
    right_side(1)
    forward(1)
    backward(1, send_two)
    parts = solved(1)
    send_edges(1, parts)
    wait_sides(0)
    for c, _, came in edges[:3 * len(dirs)]:
        when(came, c.wait_recv)
    total = acc[...] + apply(3, parts)
    for side in range(2):
        total += apply(1 + side, split2(jnp.concatenate([halo_one[side, 0], halo_one[side, 1]], axis=1)))
    total += apply_tile(0)
    for c, _, came in edges[3 * len(dirs):]:
        when(came, c.wait_recv)
    total += apply_tile(1)
    wait_sides(1)
    total += apply(4, split2(jnp.concatenate([halo_two[0], halo_two[1]], axis=1)))

    front, back = total[:256], split2(total[256:])
    row, lane = iota((OUT, DATES), 0), iota((OUT, DATES), 1)
    turned = one((row < HALF) & (row == DATES - 1 - lane)).astype(BF16)
    later = dot_nn(back[0], turned) + dot_nn(back[1], turned)
    out_ref[...] = later
    out_ref[:, 0:LANES] = front[:, 0:LANES]
    tail = front[:, LANES:OUT]
    out_ref[:, LANES:OUT] = later[:, LANES:OUT] + jnp.where(iota(tail.shape, 1) < HALF - LANES, tail, 0.0)

    def drain(k, _):
        for i in range(3):
            exchange(i, k, me).wait_send()
        return _

    lax.fori_loop(1, count, drain, 0)
    for has, group in ((has_left, sides[0]), (has_right, sides[1])):
        for c in group:
            pl.when(has)(c.wait_send)
    for c, went, _ in edges:
        when(went, c.wait_send)


def on_device(tiles, phases, pairs, class_weights, classes):
    own, tile_rows, cols = phases.shape
    tile_cols = classes.shape[1]
    count = cols // tile_cols
    assert tile_rows == 64 and tile_cols == 4
    if own % 16:
        more = -own % 16
        phases = jnp.pad(phases, ((0, more), (0, 0), (0, 0)))
        pairs = jnp.pad(pairs.reshape(count, own, 2), ((0, 0), (0, more), (0, 0))).reshape(-1, 2)
        class_weights = jnp.pad(class_weights.reshape(CLASSES, count, own), ((0, 0), (0, 0), (0, more))).reshape(CLASSES, -1)
        own += more
    nifg = pairs.shape[0]
    per = own // 2
    dirs = 1 if tiles == 2 else 2
    vmem = pl.BlockSpec(memory_space=pltpu.VMEM)
    copies = 8 + 6 * dirs

    corrected = pl.pallas_call(
        functools.partial(kernel, tile_rows, tiles),
        out_shape=jax.ShapeDtypeStruct((256, DATES), F32),
        in_specs=[pl.BlockSpec(memory_space=pl.ANY)] + [vmem] * 3,
        out_specs=vmem,
        scratch_shapes=[
            pltpu.VMEM((own, tile_rows, cols), F32),
            pltpu.VMEM((cols * per, LANES), F32),
            pltpu.VMEM((count, 4 * per, LANES), F32),
            pltpu.VMEM((2, 2 * ROWS, nifg // 2), BF16),
            pltpu.VMEM((4, nifg // 2, LANES), F32),
            pltpu.VMEM((2, MAXGAP + 1, 2 * ROWS, LANES), F32),
            pltpu.VMEM((MAXGAP + 1, ROWS, LANES), F32),
            pltpu.VMEM((MAXGAP + 1, ROWS, LANES), F32),
            pltpu.VMEM((5, 2, 2 * 256, 2 * LANES), BF16),
            pltpu.VMEM((dirs, 16, 2 * LANES), BF16),
            pltpu.VMEM((2, dirs, 2, 2 * 256, 48), BF16),
            pltpu.VMEM((2 * ROWS, LANES), F32),
            pltpu.VMEM((2 * ROWS, LANES), F32),
            pltpu.VMEM((4, OUT, LANES), F32),
            pltpu.VMEM((2, dirs, 16, OUT), F32),
            pltpu.VMEM((2, 2, OUT, LANES), F32),
            pltpu.VMEM((2, OUT, LANES), F32),
            pltpu.VMEM((2, dirs, 3, 16, OUT), F32),
            pltpu.VMEM((2 * 256, OUT), F32),
            pltpu.SemaphoreType.DMA((4,)),
            pltpu.SemaphoreType.DMA,
            pltpu.SemaphoreType.DMA((3, count)),
            pltpu.SemaphoreType.DMA((3, count)),
            pltpu.SemaphoreType.DMA((copies,)),
            pltpu.SemaphoreType.DMA((copies,)),
        ],
        compiler_params=pltpu.CompilerParams(
            collective_id=0, has_side_effects=True, vmem_limit_bytes=58 * 1024 * 1024
        ),
        name="invert_and_filter",
    )(phases, pairs.T, class_weights, classes.T)
    return corrected.reshape(tile_rows, tile_cols, DATES)


def solution(mesh):
    return jax.shard_map(
        functools.partial(on_device, mesh.shape["tile"]),
        mesh=mesh,
        in_specs=(P("ifg", "tile", None), P(), P(), P("tile", "ifg")),
        out_specs=P("tile", "ifg", None),
        check_vma=False,
    )
```

time: 49.1 us -> 43.7 us (0.89)
  the two profiles are of different devices: /device:TPU:10 before, /device:TPU:11 now
where the time goes in v1:
time: 43.7 us; the launch traced here: 43.4 us
  Pallas kernels  41.6 us (95%)
  local copies, waits for them, and re-layouts  1.85 us (4%)
    pallas_call x1, Pallas kernels, on_device(): pl.pallas_call(functools.partial(kernel, tile_rows, tiles), out_shape=jax...  41.6 us
    reshape x1, local copies, waits for them, and re-layouts, on_device(): return corrected.reshape(tile_rows, tile_cols, DATES)  1.85 us

profile of v1, /device:TPU:11, one launch (start us, length us, event | category | flops | bytes accessed | tf_op | source)
XLA Modules:
  0.0 43.4 jit_solution(8150683975114225572)
XLA Ops:
  0.0 41.6 %invert_and_filter.1 = f32[256,300]{1,0:T(8,128)} custom-call(f32[64,64,64]{2,1,0:T(8,128)} %phases_ref.1, s32[2,1024]{1,0:T(2,128)} %bitcast.2, f32[8,1024]{1,0:T(8,128)} %w_ref.1, s32[4,64]{1,0:T(4,128)} %bitcast.3), custom_call_target="tpu_custom_call" | custom-call | tf_op jit(solution)/shard_map/invert_and_filter/pallas_call | solution.py:508
  41.6 1.9 %reshape.3 = f32[64,4,300]{2,1,0:T(4,128)} reshape(f32[256,300]{1,0:T(8,128)} %invert_and_filter.1) | data formatting | bytes 614400 | tf_op jit(solution)/shard_map/reshape | solution.py:545

commit v2 on v1

--- a/solution.py
+++ b/solution.py
@@ -12,6 +12,7 @@
 MAXGAP = 8
 R = 3
 LANES = 128
+WIDE = 2 * LANES
 HALF = DATES // 2
 MEET = HALF - MAXGAP // 2
 LAST = MEET + MAXGAP
@@ -163,8 +164,9 @@
         first, second = ends[64 * h + 24:64 * h + 25, :], ends[64 * h + 32:64 * h + 33, :]
         front = one(inside & (row == second)) - one(inside & (row == first))
         back = one(inside & (DATES - 1.0 - row == second)) - one(inside & (DATES - 1.0 - row == first))
-        inc_ref[h, 0:ROWS, :] = front.astype(BF16)
-        inc_ref[h, ROWS:, :] = back.astype(BF16)
+        both = jnp.concatenate([front, back], axis=0).astype(BF16)
+        inc_ref[h, :, 0:half] = both
+        inc_ref[h, :, half:] = both
 
     bands(pairs_ref, w_ref, band)
     factor(band, low)
@@ -196,14 +198,14 @@
             value += jnp.where(out_c == at, straight, 0.0)
         return value if has is None else value * has
 
-    sets = [(1, None, 2, None), (-3, has_left, -2, has_left), (5, has_right, 6, has_right), (0, None, 3, None), (-1, has_left, 4, has_right)]
+    sets = [(1, None, 2, None), (0, None, 3, None), (-3, has_left, -2, has_left), (5, has_right, 6, has_right), (-1, has_left, 4, has_right)]
     for i, (a, has_a, b, has_b) in enumerate(sets):
         high, middle = split2(jnp.concatenate([column(a, has_a), column(b, has_b)], axis=1))
-        k_ref[i, 0] = high
-        k_ref[i, 1] = middle
+        for j, part in enumerate((high, high, middle)):
+            k_ref[:, (3 * i + j) * WIDE:(3 * i + j + 1) * WIDE] = part
     for d, (_, _, sent, _) in enumerate(dirs):
-        shape = (16, 2 * LANES)
-        row, lane = iota(shape, 0), iota(shape, 1)
+        shape = (16, 3 * WIDE)
+        row, lane = iota(shape, 0), iota(shape, 1) & (WIDE - 1)
         pick = ((row >> 2) == (lane >> 6)) & ((row & 3) < R) & ((lane & 63) == sent + (row & 3))
         sel_ref[d] = one(pick).astype(BF16)
     for p, columns in enumerate(PARTS):
@@ -218,12 +220,12 @@
             there = jnp.where(side == 0, has_left, jnp.where(side == 2, has_right, 1.0))
             value = value * there if has is None else value * there * one(has)
             high, middle = split2(value)
-            tile_ref[p, d, 0] = high
-            tile_ref[p, d, 1] = middle
-
-
-def kernel(tile_rows, tiles, phases_ref, pairs_ref, w_ref, cls_ref, out_ref,
-           phase, blocks, recv, inc_ref, wpx_ref, lpx_ref, band, low, k_ref, sel_ref, tile_ref,
+            for j, part in enumerate((high, high, middle)):
+                tile_ref[d, :, (2 * j + p) * 48:(2 * j + p + 1) * 48] = part
+
+
+def kernel(tile_rows, tiles, phases_ref, pairs_hbm, w_hbm, cls_hbm, out_ref,
+           pairs_ref, w_ref, cls_ref, phase, blocks, recv, inc_ref, wpx_ref, lpx_ref, band, low, k_ref, sel_ref, tile_ref,
            z_ref, y_ref, x_ref, edge, halo_one, halo_two, halo_tile, acc,
            load_sem, own_sem, all_send, all_recv, send_sem, recv_sem):
     me, core = lax.axis_index("ifg"), lax.axis_index("tile")
@@ -247,6 +249,11 @@
             loads.append(pltpu.make_async_copy(phases_ref.at[span], phase.at[span], load_sem.at[2 * i + h]))
             loads[-1].start()
 
+    small = []
+    for i, (src, dst) in enumerate(((pairs_hbm, pairs_ref), (w_hbm, w_ref), (cls_hbm, cls_ref))):
+        small.append(pltpu.make_async_copy(src, dst, load_sem.at[4 + i]))
+        small[-1].start()
+
     barrier = pltpu.get_barrier_semaphore()
 
     def greet(k, _):
@@ -280,13 +287,21 @@
             src_ref=blocks.at[pl.ds(pl.multiple_of(peer * 4 * per + at, 8), size)], dst_ref=recv.at[src, pl.ds(at, size)],
             send_sem=all_send.at[i, k], recv_sem=all_recv.at[i, k], device_id=(peer, core), device_id_type=MESH)
 
-    for group in ((0,), (1, 2)):
-        def send_blocks(k, _, group=group):
-            for i in group:
-                exchange(i, k, me).start()
-            return _
-
-        lax.fori_loop(1, count, send_blocks, 0)
+    def send_first(k, _):
+        exchange(0, k, me).start()
+        return _
+
+    def send_second(k, _, across):
+        crosses = (lax.rem(me + k, count) >= count // 2) != (me >= count // 2)
+
+        @pl.when(crosses if across else jnp.logical_not(crosses))
+        def _start():
+            exchange(1, k, me).start()
+            exchange(2, k, me).start()
+
+        return _
+
+    lax.fori_loop(1, count, send_first, 0)
     mine = pltpu.make_async_copy(blocks.at[pl.ds(pl.multiple_of(me * 4 * per, 8), 4 * per)], recv.at[me], own_sem)
     mine.start()
 
@@ -305,8 +320,11 @@
             if has is not None:
                 absent(has, halo_tile.at[p, d, 1])
 
+    for c in small:
+        c.wait()
     prepare(pairs_ref, w_ref, cls_ref, per, count, inc_ref, wpx_ref, lpx_ref, band, low)
     fill_filters(dirs, one(has_left), one(has_right), k_ref, sel_ref, tile_ref)
+    lax.fori_loop(1, count, functools.partial(send_second, across=False), 0)
     mine.wait()
 
     def take(group):
@@ -324,8 +342,8 @@
         for c in PARTS[p]:
             got = recv[:, c * per:(c + 1) * per, :].reshape(count * per, LANES)
             values.append(got * wpx_ref[c])
-        high, middle = split2(jnp.concatenate(values, axis=1))
-        a, b = [dot_nn(inc_ref[h], high) + dot_nn(inc_ref[h], middle) for h in range(2)]
+        value = jnp.concatenate(split2(jnp.concatenate(values, axis=1)), axis=0)
+        a, b = [dot_nn(inc_ref[h], value) for h in range(2)]
         for i in range(2):
             at = slice(i * LANES, (i + 1) * LANES)
             aa, ab, ba, bb = a[:ROWS, at], a[ROWS:, at], b[:ROWS, at], b[ROWS:, at]
@@ -415,7 +433,7 @@
 
     def send_edges(p, parts):
         for d, (_, has, _, _) in enumerate(dirs):
-            edge[p, d] = dot_nt(sel_ref[d], parts[0]) + (dot_nt(sel_ref[d], parts[1]) + dot_nt(sel_ref[d], parts[2]))
+            edge[p, d] = dot_nt(sel_ref[d], jnp.concatenate(parts, axis=1))
             opposite = len(dirs) - 1 - d
             got = dirs[opposite][1]
             for i, (slot, to, came) in enumerate(((1, None, None), (2, has_left, has_right), (0, has_right, has_left))):
@@ -423,14 +441,16 @@
                 edges.append((c, both(has, to), both(got, came)))
                 when(edges[-1][1], c.start)
 
-    def apply(i, parts):
-        return dot_nt(k_ref[i, 0], parts[0]) + (dot_nt(k_ref[i, 0], parts[1]) + dot_nt(k_ref[i, 1], parts[0]))
-
-    def apply_tile(p):
+    def apply(i, *values):
+        wide = [v for high, middle, *_ in values for v in (high, middle, high)]
+        return dot_nt(k_ref[:, 3 * WIDE * i:3 * WIDE * (i + len(values))], jnp.concatenate(wide, axis=1))
+
+    def apply_tile():
         total = None
         for d in range(len(dirs)):
-            high, middle = split2(halo_tile[p, d].reshape(48, OUT))
-            term = dot_nn(tile_ref[p, d, 0], high) + (dot_nn(tile_ref[p, d, 0], middle) + dot_nn(tile_ref[p, d, 1], high))
+            pair = [split2(halo_tile[p, d].reshape(48, OUT)) for p in range(2)]
+            order = [pair[0][0], pair[1][0], pair[0][1], pair[1][1], pair[0][0], pair[1][0]]
+            term = dot_nn(tile_ref[d], jnp.concatenate(order, axis=0))
             total = term if total is None else total + term
         return total
 
@@ -440,6 +460,7 @@
             pl.when(has_left)(sides[1][i].wait_recv)
 
     take((0,))
+    lax.fori_loop(1, count, functools.partial(send_second, across=True), 0)
     right_side(0)
     forward(0)
     backward(0, send_one)
@@ -456,13 +477,11 @@
     wait_sides(0)
     for c, _, came in edges[:3 * len(dirs)]:
         when(came, c.wait_recv)
-    total = acc[...] + apply(3, parts)
-    for side in range(2):
-        total += apply(1 + side, split2(jnp.concatenate([halo_one[side, 0], halo_one[side, 1]], axis=1)))
-    total += apply_tile(0)
+    beside = [split2(jnp.concatenate([halo_one[side, 0], halo_one[side, 1]], axis=1)) for side in range(2)]
+    total = acc[...] + apply(1, parts, *beside)
     for c, _, came in edges[3 * len(dirs):]:
         when(came, c.wait_recv)
-    total += apply_tile(1)
+    total += apply_tile()
     wait_sides(1)
     total += apply(4, split2(jnp.concatenate([halo_two[0], halo_two[1]], axis=1)))
 
@@ -470,10 +489,13 @@
     row, lane = iota((OUT, DATES), 0), iota((OUT, DATES), 1)
     turned = one((row < HALF) & (row == DATES - 1 - lane)).astype(BF16)
     later = dot_nn(back[0], turned) + dot_nn(back[1], turned)
-    out_ref[...] = later
-    out_ref[:, 0:LANES] = front[:, 0:LANES]
-    tail = front[:, LANES:OUT]
-    out_ref[:, LANES:OUT] = later[:, LANES:OUT] + jnp.where(iota(tail.shape, 1) < HALF - LANES, tail, 0.0)
+    tail = jnp.where(iota((256, OUT - LANES), 1) < HALF - LANES, front[:, LANES:OUT], 0.0)
+    first, second = front[:, 0:LANES], later[:, LANES:OUT] + tail
+    for r in range(tile_rows):
+        at = slice(4 * r, 4 * r + 4)
+        out_ref[r, :, 0:LANES] = first[at]
+        out_ref[r, :, LANES:DATES] = later[at, LANES:]
+        out_ref[r, :, LANES:OUT] = second[at]
 
     def drain(k, _):
         for i in range(3):
@@ -507,21 +529,24 @@
 
     corrected = pl.pallas_call(
         functools.partial(kernel, tile_rows, tiles),
-        out_shape=jax.ShapeDtypeStruct((256, DATES), F32),
-        in_specs=[pl.BlockSpec(memory_space=pl.ANY)] + [vmem] * 3,
+        out_shape=jax.ShapeDtypeStruct((tile_rows, tile_cols, DATES), F32),
+        in_specs=[pl.BlockSpec(memory_space=pltpu.HBM)] * 4,
         out_specs=vmem,
         scratch_shapes=[
+            pltpu.VMEM((2, nifg), jnp.int32),
+            pltpu.VMEM((CLASSES, nifg), F32),
+            pltpu.VMEM((tile_cols, tile_rows), jnp.int32),
             pltpu.VMEM((own, tile_rows, cols), F32),
             pltpu.VMEM((cols * per, LANES), F32),
             pltpu.VMEM((count, 4 * per, LANES), F32),
-            pltpu.VMEM((2, 2 * ROWS, nifg // 2), BF16),
+            pltpu.VMEM((2, 2 * ROWS, nifg), BF16),
             pltpu.VMEM((4, nifg // 2, LANES), F32),
             pltpu.VMEM((2, MAXGAP + 1, 2 * ROWS, LANES), F32),
             pltpu.VMEM((MAXGAP + 1, ROWS, LANES), F32),
             pltpu.VMEM((MAXGAP + 1, ROWS, LANES), F32),
-            pltpu.VMEM((5, 2, 2 * 256, 2 * LANES), BF16),
-            pltpu.VMEM((dirs, 16, 2 * LANES), BF16),
-            pltpu.VMEM((2, dirs, 2, 2 * 256, 48), BF16),
+            pltpu.VMEM((2 * 256, 15 * WIDE), BF16),
+            pltpu.VMEM((dirs, 16, 3 * WIDE), BF16),
+            pltpu.VMEM((dirs, 2 * 256, 6 * 48), BF16),
             pltpu.VMEM((2 * ROWS, LANES), F32),
             pltpu.VMEM((2 * ROWS, LANES), F32),
             pltpu.VMEM((4, OUT, LANES), F32),
@@ -530,7 +555,7 @@
             pltpu.VMEM((2, OUT, LANES), F32),
             pltpu.VMEM((2, dirs, 3, 16, OUT), F32),
             pltpu.VMEM((2 * 256, OUT), F32),
-            pltpu.SemaphoreType.DMA((4,)),
+            pltpu.SemaphoreType.DMA((7,)),
             pltpu.SemaphoreType.DMA,
             pltpu.SemaphoreType.DMA((3, count)),
             pltpu.SemaphoreType.DMA((3, count)),
@@ -542,7 +567,7 @@
         ),
         name="invert_and_filter",
     )(phases, pairs.T, class_weights, classes.T)
-    return corrected.reshape(tile_rows, tile_cols, DATES)
+    return corrected
 
 
 def solution(mesh):

time: 43.7 us -> 41.2 us (0.943)
  Pallas kernels: 41.6 us -> 39.3 us
    pallas_call x1, Pallas kernels: 41.6 us -> 39.3 us  [on_device(): pl.pallas_call(functools.partial(kernel, tile_rows, tiles), out_shape=jax...]
    reshape x1 -> x0, local copies, waits for them, and re-layouts: 1.85 us -> none  [on_device(): return corrected.reshape(tile_rows, tile_cols, DATES)]
    unnamed x0 -> x1, local copies, waits for them, and re-layouts: none -> 1.78 us
where the time goes in v2:
time: 41.2 us; the launch traced here: 41.1 us
  Pallas kernels  39.3 us (95%)
  local copies, waits for them, and re-layouts  1.78 us (4%)
    pallas_call x1, Pallas kernels, on_device(): pl.pallas_call(functools.partial(kernel, tile_rows, tiles), out_shape=jax...  39.3 us
    unnamed x1, local copies, waits for them, and re-layouts  1.78 us

profile of v2, /device:TPU:11, one launch (start us, length us, event | category | flops | bytes accessed | tf_op | source)
XLA Modules:
  0.0 41.1 jit_solution(169474879998877177)
XLA Ops:
  0.0 39.3 %invert_and_filter.1 = f32[64,4,300]{2,1,0:T(4,128)} custom-call(f32[64,64,64]{2,1,0:T(8,128)} %phases_ref.1, s32[2,1024]{1,0:T(2,128)} %bitcast.2, f32[8,1024]{1,0:T(8,128)} %w_hbm.1, s32[4,64]{1,0:T(4,128)} %bitcast.3), custom_call_target="tpu_custom_call" | custom-call | tf_op jit(solution)/shard_map/invert_and_filter/pallas_call | solution.py:530
  39.3 1.8 %copy.6 = f32[64,4,300]{2,1,0:T(4,128)} copy(f32[64,4,300]{2,1,0:T(4,128)} %invert_and_filter.1) | data formatting | bytes 614400

commit v3 on v2

--- a/solution.py
+++ b/solution.py
@@ -21,6 +21,7 @@
 CUT = (OUT // 16) * 8
 BLOCKS = MEET // 8
 PARTS = ((1, 2), (0, 3))
+GROUPS = ((1,), (2,), (0, 3))
 MESH = pl.DeviceIdType.MESH
 
 smooth_weight = 1.0
@@ -66,6 +67,10 @@
 
 def tap_at(delta):
     return math.exp(-delta * delta / 4.5) / NORM if abs(delta) <= R else 0.0
+
+
+def spread(start, size, stride):
+    return pl.ds(start, size, stride=stride) if stride > 1 else pl.ds(start, size)
 
 
 def swap(value):
@@ -136,25 +141,31 @@
         acc = step(pl.ds(t, 1), acc)
 
 
-def prepare(pairs_ref, w_ref, cls_ref, per, count, inc_ref, wpx_ref, lpx_ref, band, low):
+def prepare(pairs_ref, w_ref, cls_ref, await_theirs, theirs_ref, per, count, inc_ref, wpx_ref, lpx_ref, band, low):
     nifg = pairs_ref.shape[1]
     half = nifg // 2
     q, lane = iota((LANES, LANES), 0), iota((LANES, LANES), 1)
     local = q & 63
     place = (local < 3 * CLASSES) & ((q >= 64) == (lane >= 64))
-    classes = cls_ref[...]
-    classes = jnp.concatenate([classes, classes], axis=1)
-    onehot = [one(place & ((local & 7) == classes[c:c + 1, :])) for c in range(4)]
-    onehot = jnp.concatenate(onehot, axis=1).astype(BF16)
+
+    def members(ref, columns):
+        classes = ref[...]
+        classes = jnp.concatenate([classes, classes], axis=1)
+        each = [one(place & ((local & 7) == classes[c:c + 1, :])) for c in columns]
+        return jnp.concatenate(each, axis=1).astype(BF16)
+
+    onehot = members(cls_ref, range(4))
 
     parts = [p.astype(F32) for p in split3(w_ref[...])]
     ends = [jnp.broadcast_to(pairs_ref[i:i + 1, :].astype(F32), (8, nifg)) for i in range(2)]
     stack = jnp.concatenate(parts + ends + [jnp.zeros((24, nifg), F32)], axis=0)
     by_ifg = jnp.concatenate([stack, stack], axis=0).T.reshape(count, 2 * per, LANES)
-    ours, theirs = by_ifg[:, :per].reshape(half, LANES), by_ifg[:, per:].reshape(half, LANES)
-    packed = jnp.where(iota((half, LANES), 1) < 64, ours, theirs)
-    weights = dot_nn(packed.astype(BF16), onehot)
-    for c in range(4):
+    ours, others = by_ifg[:, :per].reshape(half, LANES), by_ifg[:, per:].reshape(half, LANES)
+    packed = jnp.where(iota((half, LANES), 1) < 64, ours, others)
+    await_theirs()
+    every = jnp.concatenate([onehot, members(theirs_ref, PARTS[1])], axis=1)
+    weights = dot_nn(packed.astype(BF16), every)
+    for c in range(6):
         wpx_ref[c] = weights[:, c * LANES:(c + 1) * LANES]
     ends = packed.T
     row = iota((ROWS, half), 0)
@@ -176,9 +187,9 @@
         high, middle, rest = [p.astype(F32) for p in split3(jnp.where(used & valid, low[g], 0.0))]
         value = high + pltpu.roll(middle, 8, 1) + pltpu.roll(rest, 16, 1)
         each = dot_nn(value.astype(BF16), onehot)
-        for p, columns in enumerate(PARTS):
+        for p, columns in enumerate(GROUPS):
             for i, c in enumerate(columns):
-                lpx_ref[p, g, pl.ds(i, ROWS, stride=2), :] = each[:, c * LANES:(c + 1) * LANES]
+                lpx_ref[p, g, spread(i, ROWS, len(columns)), :] = each[:, c * LANES:(c + 1) * LANES]
 
 
 def fill_filters(dirs, has_left, has_right, k_ref, sel_ref, tile_ref):
@@ -226,8 +237,8 @@
 
 def kernel(tile_rows, tiles, phases_ref, pairs_hbm, w_hbm, cls_hbm, out_ref,
            pairs_ref, w_ref, cls_ref, phase, blocks, recv, inc_ref, wpx_ref, lpx_ref, band, low, k_ref, sel_ref, tile_ref,
-           z_ref, y_ref, x_ref, edge, halo_one, halo_two, halo_tile, acc,
-           load_sem, own_sem, all_send, all_recv, send_sem, recv_sem):
+           z_ref, z_sent, z_got, theirs_ref, y_ref, x_ref, edge, halo_one, halo_two, halo_tile, acc,
+           load_sem, own_sem, first_send, first_recv, near_send, near_recv, pair_send, pair_recv, send_sem, recv_sem):
     me, core = lax.axis_index("ifg"), lax.axis_index("tile")
     count = lax.axis_size("ifg")
     own = phase.shape[0]
@@ -278,32 +289,68 @@
         lax.fori_loop(i * (per // pieces), (i + 1) * (per // pieces), turn, 0, unroll=4)
     pl.semaphore_wait(barrier, count - 1 + 3 * len(dirs))
 
-    spans = [(per, 2 * per), (0, per), (3 * per, per)]
-
-    def exchange(i, k, src):
-        peer = lax.rem(me + k, count)
-        at, size = spans[i]
-        return pltpu.make_async_remote_copy(
-            src_ref=blocks.at[pl.ds(pl.multiple_of(peer * 4 * per + at, 8), size)], dst_ref=recv.at[src, pl.ds(at, size)],
-            send_sem=all_send.at[i, k], recv_sem=all_recv.at[i, k], device_id=(peer, core), device_id_type=MESH)
-
-    def send_first(k, _):
-        exchange(0, k, me).start()
-        return _
-
-    def send_second(k, _, across):
-        crosses = (lax.rem(me + k, count) >= count // 2) != (me >= count // 2)
-
-        @pl.when(crosses if across else jnp.logical_not(crosses))
-        def _start():
-            exchange(1, k, me).start()
-            exchange(2, k, me).start()
-
-        return _
-
-    lax.fori_loop(1, count, send_first, 0)
-    mine = pltpu.make_async_copy(blocks.at[pl.ds(pl.multiple_of(me * 4 * per, 8), 4 * per)], recv.at[me], own_sem)
-    mine.start()
+    half = count // 2
+    base = jnp.where(me >= half, half, 0)
+    away = half - base
+    place = me - base
+    partner = away + place
+
+    def remote(src, dst, send, recv_at, device):
+        return pltpu.make_async_remote_copy(src_ref=src, dst_ref=dst, send_sem=send, recv_sem=recv_at,
+                                            device_id=(device, core), device_id_type=MESH)
+
+    def block_of(owner, at, size):
+        return blocks.at[pl.ds(pl.multiple_of(owner * 4 * per + at, 8), size)]
+
+    def first_copy(j, far, src, c):
+        start, i = (away, j) if far else (base, half + j)
+        peer = start + lax.rem(place + j, half)
+        return remote(block_of(peer, c * per, per), recv.at[src, pl.ds(c * per, per)], first_send.at[c - 1, i], first_recv.at[c - 1, i], peer)
+
+    def near_copy(i, j, src):
+        peer = lax.rem(place + j, half)
+        at = 3 * per * (i % 2)
+        owner, slot = (base + peer, base + src) if i < 2 else (away + peer, away + src)
+        return remote(block_of(owner, at, per), recv.at[slot, pl.ds(at, per)], near_send.at[i, j], near_recv.at[i, j], base + peer)
+
+    def each(begin, action):
+        def body(j, _):
+            action(j)
+            return _
+
+        lax.fori_loop(begin, half, body, 0)
+
+    def source(j):
+        return lax.rem(place + half - j, half)
+
+    def near_start(kinds):
+        def action(j):
+            for i in kinds:
+                near_copy(i, j, place).start()
+
+        each(1, action)
+
+    def near_wait(kinds):
+        def action(j):
+            for i in kinds:
+                near_copy(i, j, source(j)).wait_recv()
+
+        each(1, action)
+
+    theirs = remote(cls_ref, theirs_ref, pair_send.at[2], pair_recv.at[2], partner)
+    small[2].wait()
+    theirs.start()
+    each(0, lambda j: first_copy(j, True, me, 1).start())
+    each(1, lambda j: first_copy(j, False, me, 1).start())
+    near_start((2, 3))
+    each(0, lambda j: first_copy(j, True, me, 2).start())
+    each(1, lambda j: first_copy(j, False, me, 2).start())
+    mine = [pltpu.make_async_copy(block_of(me, 0, 4 * per), recv.at[me], own_sem.at[0])]
+    for i in range(2):
+        at = 3 * per * i
+        mine.append(pltpu.make_async_copy(block_of(partner, at, per), recv.at[partner, pl.ds(at, per)], own_sem.at[1 + i]))
+    for c in mine:
+        c.start()
 
     def absent(cond, *refs):
         @pl.when(jnp.logical_not(cond))
@@ -320,67 +367,78 @@
             if has is not None:
                 absent(has, halo_tile.at[p, d, 1])
 
-    for c in small:
+    for c in small[:2]:
         c.wait()
-    prepare(pairs_ref, w_ref, cls_ref, per, count, inc_ref, wpx_ref, lpx_ref, band, low)
+    prepare(pairs_ref, w_ref, cls_ref, theirs.wait_recv, theirs_ref, per, count, inc_ref, wpx_ref, lpx_ref, band, low)
     fill_filters(dirs, one(has_left), one(has_right), k_ref, sel_ref, tile_ref)
-    lax.fori_loop(1, count, functools.partial(send_second, across=False), 0)
-    mine.wait()
-
-    def take(group):
-        def take_blocks(k, _):
-            for i in group:
-                exchange(i, k, lax.rem(me + count - k, count)).wait_recv()
-            return _
-
-        lax.fori_loop(1, count, take_blocks, 0)
+    for c in mine:
+        c.wait()
+
+    def take_first(c):
+        each(0, lambda j: first_copy(j, True, away + source(j), c).wait_recv())
+        each(1, lambda j: first_copy(j, False, base + source(j), c).wait_recv())
 
     low_lanes = iota((ROWS, LANES), 1) < LANES // 2
 
-    def right_side(p):
-        values = []
-        for c in PARTS[p]:
-            got = recv[:, c * per:(c + 1) * per, :].reshape(count * per, LANES)
-            values.append(got * wpx_ref[c])
+    def sums(values, left_sides):
         value = jnp.concatenate(split2(jnp.concatenate(values, axis=1)), axis=0)
-        a, b = [dot_nn(inc_ref[h], value) for h in range(2)]
-        for i in range(2):
+        a, b = [dot_nn(side, value) for side in left_sides]
+        packed = []
+        for i in range(len(values)):
             at = slice(i * LANES, (i + 1) * LANES)
             aa, ab, ba, bb = a[:ROWS, at], a[ROWS:, at], b[:ROWS, at], b[ROWS:, at]
-            z_ref[pl.ds(i, ROWS, stride=2), :] = jnp.where(low_lanes, aa, bb) + swap(jnp.where(low_lanes, ab, ba))
+            packed.append(jnp.where(low_lanes, aa, bb) + swap(jnp.where(low_lanes, ab, ba)))
+        return packed
+
+    def first_side(c):
+        value = recv[:, c * per:(c + 1) * per, :].reshape(count * per, LANES) * wpx_ref[c]
+        z_ref[0:ROWS, :] = sums([value], [inc_ref[h] for h in range(2)])[0]
+
+    def half_side(slots, weights):
+        size = half * per
+        span = pl.ds(pl.multiple_of(base * per, LANES), size)
+        values = []
+        for c, w in zip(PARTS[1], weights):
+            got = recv[pl.ds(slots, half), c * per:(c + 1) * per, :].reshape(size, LANES)
+            values.append(got * wpx_ref[w, span, :])
+        sides = [inc_ref[h, :, span] for h in range(2)]
+        return sums(values, [jnp.concatenate([side, side], axis=1) for side in sides])
 
     def forward(p):
+        n = len(GROUPS[p])
+
         def step(t, a):
-            at = pl.ds(t, 2)
+            at = pl.ds(t, n)
             y = a[0]
             y_ref[at, :] = y * lpx_ref[p, 0, at, :]
             return [v - lpx_ref[p, j + 1, at, :] * y for j, v in enumerate(a[1:])]
 
         def block(b, carry):
             a = list(carry)
-            base = pl.multiple_of(b * 16, 16)
+            base = pl.multiple_of(b * 8 * n, 8 * n)
             for s in range(8):
-                a = step(base + 2 * s, a + [z_ref[pl.ds(base + 2 * s + 16, 2), :]])
+                a = step(base + n * s, a + [z_ref[pl.ds(base + n * (s + 8), n), :]])
             return tuple(a)
 
-        a = list(lax.fori_loop(0, BLOCKS, block, tuple(z_ref[2 * t:2 * t + 2, :] for t in range(8))))
+        a = list(lax.fori_loop(0, BLOCKS, block, tuple(z_ref[n * t:n * t + n, :] for t in range(8))))
         for t in range(8 * BLOCKS, MEET):
-            a = step(2 * t, a + [z_ref[2 * t + 16:2 * t + 18, :]])
+            a = step(n * t, a + [z_ref[n * (t + 8):n * (t + 9), :]])
         a = [a[j] + swap(a[7 - j]) for j in range(8)]
         for t in range(MEET, LAST):
-            a = step(2 * t, a)
+            a = step(n * t, a)
 
     def backward(p, send):
-        one_ref, two_ref = x_ref.at[PARTS[p][0]], x_ref.at[PARTS[p][1]]
+        n = len(GROUPS[p])
+        refs = [x_ref.at[c] for c in GROUPS[p]]
 
         def step(t, later, keep=True):
-            at = pl.ds(2 * t, 2)
+            at = pl.ds(n * t, n)
             value = y_ref[at, :]
             for g in range(len(later), 0, -1):
                 value = value - lpx_ref[p, g, at, :] * later[g - 1]
             if keep:
-                one_ref[pl.ds(t, 1), :] = value[0:1]
-                two_ref[pl.ds(t, 1), :] = value[1:2]
+                for i, ref in enumerate(refs):
+                    ref[pl.ds(t, 1), :] = value[i:i + 1]
             return [value] + later[:7]
 
         later = []
@@ -406,16 +464,20 @@
 
     sides = [[], []]
 
-    def send_one(piece, span):
-        src = x_ref.at[pl.ds(1, 2), span]
-        sides[0].append(copy(2 * piece, src, halo_one.at[1, :, span], (left, core)))
-        sides[1].append(copy(2 * piece + 1, src, halo_one.at[0, :, span], (right, core)))
-        pl.when(has_left)(sides[0][-1].start)
-        pl.when(has_right)(sides[1][-1].start)
+    def send_one(c):
+        def send(piece, span):
+            at = 4 * (c - 1) + 2 * piece
+            src = x_ref.at[c, span]
+            sides[0].append(copy(at, src, halo_one.at[1, c - 1, span], (left, core)))
+            sides[1].append(copy(at + 1, src, halo_one.at[0, c - 1, span], (right, core)))
+            pl.when(has_left)(sides[0][-1].start)
+            pl.when(has_right)(sides[1][-1].start)
+
+        return send
 
     def send_two(piece, span):
-        sides[0].append(copy(4 + 2 * piece, x_ref.at[0, span], halo_two.at[1, span], (left, core)))
-        sides[1].append(copy(5 + 2 * piece, x_ref.at[3, span], halo_two.at[0, span], (right, core)))
+        sides[0].append(copy(8 + 2 * piece, x_ref.at[0, span], halo_two.at[1, span], (left, core)))
+        sides[1].append(copy(9 + 2 * piece, x_ref.at[3, span], halo_two.at[0, span], (right, core)))
         pl.when(has_left)(sides[0][-1].start)
         pl.when(has_right)(sides[1][-1].start)
 
@@ -437,7 +499,7 @@
             opposite = len(dirs) - 1 - d
             got = dirs[opposite][1]
             for i, (slot, to, came) in enumerate(((1, None, None), (2, has_left, has_right), (0, has_right, has_left))):
-                c = copy(8 + (p * len(dirs) + d) * 3 + i, edge.at[p, d], halo_tile.at[p, opposite, slot], near[d][i])
+                c = copy(12 + (p * len(dirs) + d) * 3 + i, edge.at[p, d], halo_tile.at[p, opposite, slot], near[d][i])
                 edges.append((c, both(has, to), both(got, came)))
                 when(edges[-1][1], c.start)
 
@@ -454,27 +516,41 @@
             total = term if total is None else total + term
         return total
 
-    def wait_sides(first):
-        for i in (2 * first, 2 * first + 1):
+    def wait_sides(begin, end):
+        for i in range(begin, end):
             pl.when(has_right)(sides[0][i].wait_recv)
             pl.when(has_left)(sides[1][i].wait_recv)
 
-    take((0,))
-    lax.fori_loop(1, count, functools.partial(send_second, across=True), 0)
-    right_side(0)
+    take_first(1)
+    first_side(1)
     forward(0)
-    backward(0, send_one)
+    backward(0, send_one(1))
+    near_start((0, 1))
+    near_wait((2, 3))
+    for i, z in enumerate(half_side(away, (4, 5))):
+        z_sent[i] = z[:OUT]
+    summed = [remote(z_sent.at[i], z_got.at[i], pair_send.at[i], pair_recv.at[i], partner) for i in range(2)]
+    take_first(2)
+    for c in summed:
+        c.start()
+    first_side(2)
+    forward(1)
+    backward(1, send_one(2))
     parts = solved(0)
     send_edges(0, parts)
     acc[...] = apply(0, parts)
 
-    take((1, 2))
-    right_side(1)
-    forward(1)
-    backward(1, send_two)
+    near_wait((0, 1))
+    nearby = half_side(base, PARTS[1])
+    for i, z in enumerate(nearby):
+        summed[i].wait_recv()
+        z_ref[pl.ds(i, OUT, stride=2), :] = z[:OUT] + z_got[i]
+        z_ref[pl.ds(2 * OUT + i, ROWS - OUT, stride=2), :] = z[OUT:]
+    forward(2)
+    backward(2, send_two)
     parts = solved(1)
     send_edges(1, parts)
-    wait_sides(0)
+    wait_sides(0, 4)
     for c, _, came in edges[:3 * len(dirs)]:
         when(came, c.wait_recv)
     beside = [split2(jnp.concatenate([halo_one[side, 0], halo_one[side, 1]], axis=1)) for side in range(2)]
@@ -482,7 +558,7 @@
     for c, _, came in edges[3 * len(dirs):]:
         when(came, c.wait_recv)
     total += apply_tile()
-    wait_sides(1)
+    wait_sides(4, 6)
     total += apply(4, split2(jnp.concatenate([halo_two[0], halo_two[1]], axis=1)))
 
     front, back = total[:256], split2(total[256:])
@@ -497,12 +573,17 @@
         out_ref[r, :, LANES:DATES] = later[at, LANES:]
         out_ref[r, :, LANES:OUT] = second[at]
 
-    def drain(k, _):
-        for i in range(3):
-            exchange(i, k, me).wait_send()
-        return _
-
-    lax.fori_loop(1, count, drain, 0)
+    def sent(j, far):
+        for c in PARTS[0]:
+            first_copy(j, far, me, c).wait_send()
+        if not far:
+            for i in range(4):
+                near_copy(i, j, place).wait_send()
+
+    each(0, functools.partial(sent, far=True))
+    each(1, functools.partial(sent, far=False))
+    for c in [theirs] + summed:
+        c.wait_send()
     for has, group in ((has_left, sides[0]), (has_right, sides[1])):
         for c in group:
             pl.when(has)(c.wait_send)
@@ -514,7 +595,7 @@
     own, tile_rows, cols = phases.shape
     tile_cols = classes.shape[1]
     count = cols // tile_cols
-    assert tile_rows == 64 and tile_cols == 4
+    assert tile_rows == 64 and tile_cols == 4 and count % 2 == 0
     if own % 16:
         more = -own % 16
         phases = jnp.pad(phases, ((0, more), (0, 0), (0, 0)))
@@ -525,7 +606,7 @@
     per = own // 2
     dirs = 1 if tiles == 2 else 2
     vmem = pl.BlockSpec(memory_space=pltpu.VMEM)
-    copies = 8 + 6 * dirs
+    copies = 12 + 6 * dirs
 
     corrected = pl.pallas_call(
         functools.partial(kernel, tile_rows, tiles),
@@ -540,14 +621,17 @@
             pltpu.VMEM((cols * per, LANES), F32),
             pltpu.VMEM((count, 4 * per, LANES), F32),
             pltpu.VMEM((2, 2 * ROWS, nifg), BF16),
-            pltpu.VMEM((4, nifg // 2, LANES), F32),
-            pltpu.VMEM((2, MAXGAP + 1, 2 * ROWS, LANES), F32),
+            pltpu.VMEM((6, nifg // 2, LANES), F32),
+            pltpu.VMEM((3, MAXGAP + 1, 2 * ROWS, LANES), F32),
             pltpu.VMEM((MAXGAP + 1, ROWS, LANES), F32),
             pltpu.VMEM((MAXGAP + 1, ROWS, LANES), F32),
             pltpu.VMEM((2 * 256, 15 * WIDE), BF16),
             pltpu.VMEM((dirs, 16, 3 * WIDE), BF16),
             pltpu.VMEM((dirs, 2 * 256, 6 * 48), BF16),
             pltpu.VMEM((2 * ROWS, LANES), F32),
+            pltpu.VMEM((2, OUT, LANES), F32),
+            pltpu.VMEM((2, OUT, LANES), F32),
+            pltpu.VMEM((tile_cols, tile_rows), jnp.int32),
             pltpu.VMEM((2 * ROWS, LANES), F32),
             pltpu.VMEM((4, OUT, LANES), F32),
             pltpu.VMEM((2, dirs, 16, OUT), F32),
@@ -556,9 +640,13 @@
             pltpu.VMEM((2, dirs, 3, 16, OUT), F32),
             pltpu.VMEM((2 * 256, OUT), F32),
             pltpu.SemaphoreType.DMA((7,)),
-            pltpu.SemaphoreType.DMA,
-            pltpu.SemaphoreType.DMA((3, count)),
-            pltpu.SemaphoreType.DMA((3, count)),
+            pltpu.SemaphoreType.DMA((3,)),
+            pltpu.SemaphoreType.DMA((2, count)),
+            pltpu.SemaphoreType.DMA((2, count)),
+            pltpu.SemaphoreType.DMA((4, count // 2)),
+            pltpu.SemaphoreType.DMA((4, count // 2)),
+            pltpu.SemaphoreType.DMA((3,)),
+            pltpu.SemaphoreType.DMA((3,)),
             pltpu.SemaphoreType.DMA((copies,)),
             pltpu.SemaphoreType.DMA((copies,)),
         ],

time: 41.2 us -> 38.3 us (0.930)
  the two profiles are of different devices: /device:TPU:11 before, /device:TPU:1 now
where the time goes in v3:
time: 38.3 us; the launch traced here: 38.2 us
  Pallas kernels  36.4 us (95%)
  local copies, waits for them, and re-layouts  1.78 us (5%)
    pallas_call x1, Pallas kernels, on_device(): pl.pallas_call(functools.partial(kernel, tile_rows, tiles), out_shape=jax...  36.4 us
    unnamed x1, local copies, waits for them, and re-layouts  1.78 us

profile of v3, /device:TPU:1, one launch (start us, length us, event | category | flops | bytes accessed | tf_op | source)
XLA Modules:
  0.0 38.2 jit_solution(2295440654427696859)
XLA Ops:
  0.0 36.4 %invert_and_filter.1 = f32[64,4,300]{2,1,0:T(4,128)} custom-call(f32[64,64,64]{2,1,0:T(8,128)} %phases_ref.1, s32[2,1024]{1,0:T(2,128)} %bitcast.2, f32[8,1024]{1,0:T(8,128)} %w_hbm.1, s32[4,64]{1,0:T(4,128)} %bitcast.3), custom_call_target="tpu_custom_call" | custom-call | tf_op jit(solution)/shard_map/invert_and_filter/pallas_call | solution.py:611
  36.4 1.8 %copy.6 = f32[64,4,300]{2,1,0:T(4,128)} copy(f32[64,4,300]{2,1,0:T(4,128)} %invert_and_filter.1) | data formatting | bytes 614400

commit v4 on v3

--- a/solution.py
+++ b/solution.py
@@ -252,7 +252,7 @@
         dirs = [(lax.rem(core + tiles - 1, tiles), core > 0, 0, -R),
                 (lax.rem(core + 1, tiles), core < tiles - 1, tile_rows - R, tile_rows)]
 
-    pieces = 2
+    pieces = 4
     loads = []
     for i in range(pieces):
         for h in range(2):
@@ -262,7 +262,7 @@
 
     small = []
     for i, (src, dst) in enumerate(((pairs_hbm, pairs_ref), (w_hbm, w_ref), (cls_hbm, cls_ref))):
-        small.append(pltpu.make_async_copy(src, dst, load_sem.at[4 + i]))
+        small.append(pltpu.make_async_copy(src, dst, load_sem.at[8 + i]))
         small[-1].start()
 
     barrier = pltpu.get_barrier_semaphore()
@@ -525,14 +525,14 @@
     first_side(1)
     forward(0)
     backward(0, send_one(1))
-    near_start((0, 1))
     near_wait((2, 3))
     for i, z in enumerate(half_side(away, (4, 5))):
         z_sent[i] = z[:OUT]
     summed = [remote(z_sent.at[i], z_got.at[i], pair_send.at[i], pair_recv.at[i], partner) for i in range(2)]
-    take_first(2)
     for c in summed:
         c.start()
+    near_start((0, 1))
+    take_first(2)
     first_side(2)
     forward(1)
     backward(1, send_one(2))
@@ -639,7 +639,7 @@
             pltpu.VMEM((2, OUT, LANES), F32),
             pltpu.VMEM((2, dirs, 3, 16, OUT), F32),
             pltpu.VMEM((2 * 256, OUT), F32),
-            pltpu.SemaphoreType.DMA((7,)),
+            pltpu.SemaphoreType.DMA((11,)),
             pltpu.SemaphoreType.DMA((3,)),
             pltpu.SemaphoreType.DMA((2, count)),
             pltpu.SemaphoreType.DMA((2, count)),

time: 38.3 us -> 37.8 us (0.987)
  Pallas kernels: 36.4 us -> 35.9 us
    pallas_call x1, Pallas kernels: 36.4 us -> 35.9 us  [on_device(): pl.pallas_call(functools.partial(kernel, tile_rows, tiles), out_shape=jax...]
where the time goes in v4:
time: 37.8 us; the launch traced here: 37.7 us
  Pallas kernels  35.9 us (95%)
  local copies, waits for them, and re-layouts  1.78 us (5%)
    pallas_call x1, Pallas kernels, on_device(): pl.pallas_call(functools.partial(kernel, tile_rows, tiles), out_shape=jax...  35.9 us
    unnamed x1, local copies, waits for them, and re-layouts  1.78 us

profile of v4, /device:TPU:1, one launch (start us, length us, event | category | flops | bytes accessed | tf_op | source)
XLA Modules:
  0.0 37.7 jit_solution(5655126432119112905)
XLA Ops:
  0.0 35.9 %invert_and_filter.1 = f32[64,4,300]{2,1,0:T(4,128)} custom-call(f32[64,64,64]{2,1,0:T(8,128)} %phases_ref.1, s32[2,1024]{1,0:T(2,128)} %bitcast.2, f32[8,1024]{1,0:T(8,128)} %w_hbm.1, s32[4,64]{1,0:T(4,128)} %bitcast.3), custom_call_target="tpu_custom_call" | custom-call | tf_op jit(solution)/shard_map/invert_and_filter/pallas_call | solution.py:611
  35.9 1.8 %copy.6 = f32[64,4,300]{2,1,0:T(4,128)} copy(f32[64,4,300]{2,1,0:T(4,128)} %invert_and_filter.1) | data formatting | bytes 614400

commit v5 on v4

--- a/solution.py
+++ b/solution.py
@@ -340,8 +340,8 @@
     theirs = remote(cls_ref, theirs_ref, pair_send.at[2], pair_recv.at[2], partner)
     small[2].wait()
     theirs.start()
+    each(1, lambda j: first_copy(j, False, me, 1).start())
     each(0, lambda j: first_copy(j, True, me, 1).start())
-    each(1, lambda j: first_copy(j, False, me, 1).start())
     near_start((2, 3))
     each(0, lambda j: first_copy(j, True, me, 2).start())
     each(1, lambda j: first_copy(j, False, me, 2).start())
@@ -550,11 +550,12 @@
     backward(2, send_two)
     parts = solved(1)
     send_edges(1, parts)
+    acc[...] += apply(1, parts)
     wait_sides(0, 4)
     for c, _, came in edges[:3 * len(dirs)]:
         when(came, c.wait_recv)
     beside = [split2(jnp.concatenate([halo_one[side, 0], halo_one[side, 1]], axis=1)) for side in range(2)]
-    total = acc[...] + apply(1, parts, *beside)
+    total = acc[...] + apply(2, *beside)
     for c, _, came in edges[3 * len(dirs):]:
         when(came, c.wait_recv)
     total += apply_tile()

time: 37.8 us -> 37.5 us (level)
  the two profiles are of different devices: /device:TPU:1 before, /device:TPU:11 now
where the time goes in v5:
time: 37.5 us; the launch traced here: 36.9 us
  Pallas kernels  35.1 us (94%)
  local copies, waits for them, and re-layouts  1.78 us (5%)
    pallas_call x1, Pallas kernels, on_device(): pl.pallas_call(functools.partial(kernel, tile_rows, tiles), out_shape=jax...  35.1 us
    unnamed x1, local copies, waits for them, and re-layouts  1.78 us

profile of v5, /device:TPU:11, one launch (start us, length us, event | category | flops | bytes accessed | tf_op | source)
XLA Modules:
  0.0 36.9 jit_solution(2743169265769963613)
XLA Ops:
  0.0 35.1 %invert_and_filter.1 = f32[64,4,300]{2,1,0:T(4,128)} custom-call(f32[64,64,64]{2,1,0:T(8,128)} %phases_ref.1, s32[2,1024]{1,0:T(2,128)} %bitcast.2, f32[8,1024]{1,0:T(8,128)} %w_hbm.1, s32[4,64]{1,0:T(4,128)} %bitcast.3), custom_call_target="tpu_custom_call" | custom-call | tf_op jit(solution)/shard_map/invert_and_filter/pallas_call | solution.py:612
  35.1 1.8 %copy.6 = f32[64,4,300]{2,1,0:T(4,128)} copy(f32[64,4,300]{2,1,0:T(4,128)} %invert_and_filter.1) | data formatting | bytes 614400
